TPU v7x, 512 devices: a whole 4x8x8 slice. The times are simulated.
512 devices in a mesh: sta: 64 (over x, y, core), day: 8 (over z).
Axes of the slice: x: 4, y: 8, z: 8, core: 2. Of those that a mesh axis runs over, the one named last changes fastest.
Arguments:
- spectra: bfloat16 [8, 4096, 512], P('day', 'sta'), may hold values from -6 to 6
- picks: int32 [64, 64, 8], P('sta'), may hold values from 0 to 63
- pair_own: int32 [65536], P('sta'), may hold values from 0 to 63
- pair_far: int32 [65536], P('sta'), may hold values from 0 to 511
- pair_mask: int32 [65536], P('sta'), may hold values 0 or 1
Outputs:
- stacks: float32 [65536, 1024], P(('sta', 'day'))
All inputs are finite; a program needn't handle non-finite values. No bound on the sum of `pair_mask` on one device may be relied on, other than what follows from the above.
Results may differ from a plain program's by a relative error of at most 0.0003.
Values may be sent and summed in bfloat16 or wider, within the bound.
No kernel may reach another device: no remote copies, remote signals or barrier semaphores. Data moves between devices by JAX's collectives and lax.ppermute only.
A program may use at most 64 MiB of HBM per device.

v0:
```python
import jax
import jax.numpy as jnp
from jax import lax
from jax.sharding import PartitionSpec as P

SLOTS = 8
LAGS = 1024


def lag_table(bins, lags, base):
    k = jnp.arange(bins)[:, None] + base
    m = jnp.arange(lags)[None, :] - lags // 2
    q = k * m % lags
    angle = 2.0 * jnp.pi / lags * q.astype(jnp.float32)
    return jnp.concatenate([jnp.cos(angle), -jnp.sin(angle)], axis=0)


def local(spectra, picks, pair_own, pair_far, pair_mask):
    n_sta = lax.axis_size("sta")
    n_day = lax.axis_size("day")
    block = spectra[0]
    width = block.shape[1]
    bins = width // 2
    chosen = jnp.take(block, picks[0].reshape(-1), axis=0).reshape(n_sta, SLOTS, width)
    received = lax.all_to_all(chosen, "sta", split_axis=0, concat_axis=0, tiled=True).reshape(
        n_sta * SLOTS, width
    )
    near = jnp.take(block, pair_own, axis=0).astype(jnp.float32)
    far_part = jnp.take(received, pair_far, axis=0).astype(jnp.float32)
    near_re, near_im = (near[:, :bins], near[:, bins:])
    far_re, far_im = (far_part[:, :bins], far_part[:, bins:])
    weight = pair_mask.astype(jnp.float32)[:, None]
    cross = weight * jnp.concatenate(
        [near_re * far_re + near_im * far_im, near_im * far_re - near_re * far_im], axis=1
    )
    table = lag_table(bins, LAGS, LAGS // 25)
    scale = 1.0 / jnp.sqrt(jnp.float32(2 * bins * n_day))
    summed = lax.psum_scatter(cross, "day", scatter_dimension=0, tiled=True)
    stacks = (
        jnp.dot(summed, table, precision=lax.Precision.HIGHEST, preferred_element_type=jnp.float32)
        * scale
    )
    return stacks


def solution(mesh):
    in_specs = (P("day", "sta", None), P("sta", None, None), P("sta"), P("sta"), P("sta"))
    out_specs = P(("sta", "day"), None)
    return jax.shard_map(local, mesh=mesh, in_specs=in_specs, out_specs=out_specs, check_vma=False)
```

profile of v0, /device:TPU:6, one launch (start us, length us, event | category | flops | bytes accessed | tf_op | source)
XLA Modules:
  0.0 103.6 jit_solution(12714422695772522682)
XLA Ops:
  6.5 0.0 copy-start
  6.5 0.8 copy.8
  7.3 0.7 compare_and_fusion
  8.0 0.1 reshape_squeeze.6
  8.1 0.1 copy.7
  8.3 0.0 copy-done
  8.3 2.0 %gather_fusion.1 = bf16[512,512]{1,0:T(8,128)(2,1)S(1)} fusion(bf16[64,512]{1,0:T(8,128)(2,1)S(1)} %bitcast.11, s32[1024]{0:T(1024)S(1)} %pad_clamp_fusion), kind=kCustom, calls=%fused_computation.1 | custom fusion | bytes 1050624 | tf_op jit(solution)/shard_map/jit(_take)/gather | solution.py:24
  10.2 0.0 copy-start.1
  10.2 0.9 bitcast_select_fusion
  11.2 10.8 %all-to-all-start = ((bf16[64,8,512]{2,1,0:T(8,128)(2,1)}), bf16[64,8,512]{2,1,0:T(8,128)(2,1)S(1)}, u32[]{:S(2)}, u32[]{:S(2)}) async-start(bf16[64,8,512]{2,1,0:T(8,128)(2,1)} %bitcast_select_fusion), calls=%async_computation | async-start | bytes 1048576 | tf_op jit(solution)/shard_map/all_to_all | solution.py:25
  22.0 0.0 reduce-scatter.2.cloned.1.call-start
  22.1 0.0 copy-start.3
  22.1 0.0 copy-start.2
  22.1 5.1 %gather_fusion = bf16[1024,512]{1,0:T(8,128)(2,1)} fusion(bf16[64,512]{1,0:T(8,128)(2,1)S(1)} %bitcast.10, s32[1024]{0:T(1024)S(1)} %fusion.11), kind=kCustom, calls=%fused_computation | custom fusion | bytes 2101248 | tf_op jit(solution)/shard_map/jit(_take)/gather | solution.py:28
  27.2 1.4 %select_convert_fusion.1 = f32[1024,512]{1,0:T(8,128)S(1)} fusion(bf16[1024,512]{1,0:T(8,128)(2,1)} %gather_fusion, pred[1024]{0:T(1024)(128)(4,1)S(1)} %compare_and_fusion.2), kind=kLoop, calls=%fused_computation.21 | loop fusion | flops 1048576 | bytes 3146752 | tf_op jit(solution)/shard_map/convert_element_type | solution.py:28
  28.7 10.0 %all-to-all-done = bf16[64,8,512]{2,1,0:T(8,128)(2,1)S(1)} async-done(((bf16[64,8,512]{2,1,0:T(8,128)(2,1)}), bf16[64,8,512]{2,1,0:T(8,128)(2,1)S(1)}, u32[]{:S(2)}, u32[]{:S(2)}) %all-to-all-start) | async-done | bytes 524320 | tf_op jit(solution)/shard_map/all_to_all | solution.py:25
  38.7 5.1 %gather_fusion.2 = bf16[1024,512]{1,0:T(8,128)(2,1)} fusion(bf16[512,512]{1,0:T(8,128)(2,1)S(1)} %bitcast.12, s32[1024]{0:T(1024)S(1)} %fusion.12), kind=kCustom, calls=%fused_computation.2 | custom fusion | bytes 2101248 | tf_op jit(solution)/shard_map/jit(_take)/gather | solution.py:29
  43.8 1.4 %select_convert_fusion = f32[1024,512]{1,0:T(8,128)S(1)} fusion(bf16[1024,512]{1,0:T(8,128)(2,1)} %gather_fusion.2, pred[1024]{0:T(1024)(128)(4,1)S(1)} %compare_and_fusion.1), kind=kLoop, calls=%fused_computation.20 | loop fusion | flops 1048576 | bytes 3146752 | tf_op jit(solution)/shard_map/convert_element_type | solution.py:29
  45.2 0.3 multiply_add_fusion
  45.5 1.5 %maximum_multiply_fusion = f32[1024,512]{1,0:T(8,128)} fusion(f32[1024,256]{1,0:T(8,128)S(1)} %get-tuple-element.6, f32[1024,256]{1,0:T(8,128)S(1)} %get-tuple-element.5, f32[1024]{0:T(1024)S(1)} %convert_element_type.14), kind=kLoop, calls=%fused_computation.3 | loop fusion | flops 1048576 | bytes 4198400 | tf_op jit(solution)/shard_map/mul | solution.py:33
  47.1 0.0 reduce-scatter.2.cloned.1.call-update
  47.1 4.2 %fusion.10 = (f32[256,1024]{1,0:T(8,128)S(1)}, f32[256,1024]{1,0:T(8,128)S(1)}) fusion(s32[1024]{0:T(1024)S(1)} %iota_add_fusion, s32[256]{0:T(256)S(1)} %iota_add_fusion.1), kind=kLoop, calls=%fused_computation.23 | loop fusion | flops 3932160 | bytes 2102272 | tf_op jit(solution)/shard_map/cos | solution.py:15
  51.3 42.4 %reduce-scatter.2.cloned.1.call-done = f32[128,512]{1,0:T(8,128)} async-done(((f32[1024,512]{1,0:T(8,128)}), f32[128,512]{1,0:T(8,128)}) %reduce-scatter.2.cloned.1.call-update) | async-done | bytes 262160 | tf_op jit(solution)/shard_map/reduce_scatter | solution.py:38
  93.7 3.0 %fusion.4 = f32[128,1024]{1,0:T(8,128)} fusion(f32[128,512]{1,0:T(8,128)} %reduce-scatter.2.cloned.1.call-done, f32[256,1024]{1,0:T(8,128)S(1)} %get-tuple-element.8, f32[256,1024]{1,0:T(8,128)S(1)} %get-tuple-element.7), kind=kOutput, calls=%fused_computation.13 | convolution fusion | flops 805961728 | bytes 2883584 | tf_op jit(solution)/shard_map/dot_general | solution.py:40
  (12 shorter events, 0.1 us)
Async XLA Ops:
  6.5 1.7 %copy-start = (bf16[1,64,512]{2,1,0:T(8,128)(2,1)S(1)}, bf16[1,64,512]{2,1,0:T(8,128)(2,1)}, u32[]{:S(2)}) copy-start(bf16[1,64,512]{2,1,0:T(8,128)(2,1)} %param.5) | copy-start | bytes 196612
  10.2 11.8 %copy-start.1 = (s32[1024]{0:T(1024)S(1)}, s32[1024]{0:T(1024)}, u32[]{:S(2)}) copy-start(s32[1024]{0:T(1024)} %param.7) | copy-start | bytes 12292
  11.2 27.5 %all-to-all-start = ((bf16[64,8,512]{2,1,0:T(8,128)(2,1)}), bf16[64,8,512]{2,1,0:T(8,128)(2,1)S(1)}, u32[]{:S(2)}, u32[]{:S(2)}) async-start(bf16[64,8,512]{2,1,0:T(8,128)(2,1)} %bitcast_select_fusion), calls=%async_computation | async-start | bytes 1048576 | tf_op jit(solution)/shard_map/all_to_all | solution.py:25
  22.0 71.7 %reduce-scatter.2.cloned.1.call-start = ((), (), s32[]{:S(2)}) async-start(), calls=%async_computation.2 | async-start | bytes 2359296 | tf_op jit(solution)/shard_map/reduce_scatter | solution.py:38
  22.1 5.1 %copy-start.3 = (s32[1024]{0:T(1024)S(1)}, s32[1024]{0:T(1024)}, u32[]{:S(2)}) copy-start(s32[1024]{0:T(1024)} %param.9) | copy-start | bytes 12292
  22.1 5.1 %copy-start.2 = (s32[1024]{0:T(1024)S(1)}, s32[1024]{0:T(1024)}, u32[]{:S(2)}) copy-start(s32[1024]{0:T(1024)} %param.8) | copy-start | bytes 12292
Sparse Core Ops, SparseCore 0:
  47.2 46.4 reduce-scatter.1
where the time goes:
time: 104 us
  waiting for transfers between devices  52.5 us (50%)
  between operations  13.5 us (13%)
  local copies, waits for them, and re-layouts  13.1 us (13%)
  starting transfers between devices  10.8 us (10%)
  other arithmetic  10.6 us (10%)
  matrix products  3.03 us (3%)
    reduce_scatter x1, waiting for transfers between devices, local(): summed = lax.psum_scatter(cross, 'day', scatter_dimension=0, tiled=True)  42.4 us
    all_to_all x1, starting transfers between devices, local(): lax.all_to_all(chosen, 'sta', split_axis=0, concat_axis=0, tiled=True)  10.8 us
    all_to_all x1, waiting for transfers between devices, local(): lax.all_to_all(chosen, 'sta', split_axis=0, concat_axis=0, tiled=True)  10 us
    gather x1, local copies, waits for them, and re-layouts, local(): near = jnp.take(block, pair_own, axis=0).astype(jnp.float32)  5.08 us
    gather x1, local copies, waits for them, and re-layouts, local(): far_part = jnp.take(received, pair_far, axis=0).astype(jnp.float32)  5.07 us
    cos x1, other arithmetic, lag_table(): return jnp.concatenate([jnp.cos(angle), -jnp.sin(angle)], axis=0)  4.18 us
    dot_general x1, matrix products, local(): jnp.dot(summed, table, precision=lax.Precision.HIGHEST, preferred_element...  3.03 us
  transfers between devices with their start and end apart: 2, of which 2 were waited for; matrix products, arithmetic and copies ran while one was open for 10% of the time, Pallas kernels for 0%

commit v1 on v0

v1 whole, which is shorter than its diff:
```python
import jax
import jax.numpy as jnp
import numpy as np
from jax import lax
from jax.experimental import pallas as pl
from jax.experimental.pallas import tpu as pltpu
from jax.sharding import PartitionSpec as P

SLOTS = 8
LAGS = 1024
BASE = 40
BF16 = jnp.bfloat16
F32 = jnp.float32
VMEM = pl.BlockSpec(memory_space=pltpu.VMEM)


def lag_table(bins, n_day, scale):
    k = np.arange(bins)[:, None] + BASE
    m = np.arange(LAGS)[None, :] - LAGS // 2
    angle = 2.0 * np.pi / LAGS * (k * m % LAGS)
    part = bins // n_day
    both = np.stack([np.cos(angle), -np.sin(angle)]) * scale
    both = both.reshape(2, n_day, part, LAGS).transpose(1, 0, 2, 3).reshape(2 * bins, LAGS).astype(np.float32)
    high = both.astype(jnp.bfloat16)
    low = (both - high.astype(np.float32)).astype(jnp.bfloat16)
    return high, low


def turn_kernel(x_ref, out_ref):
    n_day, part, _ = out_ref.shape
    bins = n_day * part
    x = x_ref[0].astype(F32)
    y = jnp.concatenate([x[:, :bins], x[:, bins:]], axis=0)
    out_ref[...] = y.T.astype(BF16).reshape(out_ref.shape)


def pick_kernel(picks_ref, mine_ref, out_ref):
    slots, owners = picks_ref.shape
    n_day, part, twice = mine_ref.shape
    rows = n_day * part
    mine = mine_ref[...].reshape(rows, twice)
    picks = picks_ref[...]
    lane = lax.broadcasted_iota(jnp.int32, (slots, twice), 1)
    for half in range(2):
        hot = jnp.concatenate(
            [(lane == picks[:, o : o + 1] + half * (twice // 2)).astype(F32) for o in range(owners)], axis=0
        ).astype(BF16)
        got = lax.dot_general(hot, mine, (((1,), (1,)), ((), ())), preferred_element_type=F32)
        out_ref[:, :, half * rows : (half + 1) * rows] = got.astype(BF16).reshape(owners, slots, rows)


def cross_kernel(own_ref, far_ref, mask_ref, mine_ref, got_ref, out_ref, turned):
    n_day, part, twice = mine_ref.shape
    rows = n_day * part
    slots = got_ref.shape[0]
    blocks, lanes = own_ref.shape
    mine = mine_ref[...].reshape(rows, twice)
    turned[...] = got_ref[...].astype(F32).T.astype(BF16)
    near_row = lax.broadcasted_iota(jnp.int32, (twice, lanes), 0)
    far_row = lax.broadcasted_iota(jnp.int32, (slots, lanes), 0)
    for j in range(blocks):
        own = jnp.where(mask_ref[j : j + 1, :] > 0, own_ref[j : j + 1, :], 2 * twice)
        far = far_ref[j : j + 1, :]
        hot_re = (near_row == own).astype(F32).astype(BF16)
        hot_im = (near_row == own + twice // 2).astype(F32).astype(BF16)
        hot_far = (far_row == far).astype(F32).astype(BF16)
        near_re = jnp.dot(mine, hot_re, preferred_element_type=F32)
        near_im = jnp.dot(mine, hot_im, preferred_element_type=F32)
        both = jnp.dot(turned[...], hot_far, preferred_element_type=F32)
        far_re, far_im = both[:rows], both[rows:]
        real = near_re * far_re + near_im * far_im
        imag = near_im * far_re - near_re * far_im
        out_ref[j, :part, :] = jnp.sum(real.reshape(n_day, part, lanes), axis=0)
        out_ref[j, part:, :] = jnp.sum(imag.reshape(n_day, part, lanes), axis=0)


def stack_kernel(summed_ref, high_ref, low_ref, out_ref):
    turned = summed_ref[...].T
    high = turned.astype(BF16)
    low = (turned - high.astype(F32)).astype(BF16)
    out = jnp.dot(high, high_ref[...], preferred_element_type=F32)
    out += jnp.dot(low, high_ref[...], preferred_element_type=F32)
    out += jnp.dot(high, low_ref[...], preferred_element_type=F32)
    out_ref[...] = out


def call(kernel, shape, dtype, n_in, scratch=()):
    return pl.pallas_call(
        kernel,
        out_shape=jax.ShapeDtypeStruct(shape, dtype),
        in_specs=[VMEM] * n_in,
        out_specs=VMEM,
        scratch_shapes=list(scratch),
        compiler_params=pltpu.CompilerParams(vmem_limit_bytes=48 * 1024 * 1024),
    )


def local(spectra, picks, pair_own, pair_far, pair_mask):
    n_sta = lax.axis_size("sta")
    n_day = lax.axis_size("day")
    _, stations, width = spectra.shape
    bins = width // 2
    part = bins // n_day
    pairs = pair_own.shape[0]
    mine_pairs = pairs // n_day

    by_bin = call(turn_kernel, (n_day, part, 2 * stations), BF16, 1)(spectra)
    mine = lax.all_to_all(by_bin, "day", split_axis=0, concat_axis=0, tiled=True)
    chosen = call(pick_kernel, (n_sta, SLOTS, width), BF16, 2)(picks[0].T, mine)
    got = lax.all_to_all(chosen, "sta", split_axis=0, concat_axis=0, tiled=True).reshape(n_sta * SLOTS, width)
    by_block = [a.reshape(n_day, mine_pairs) for a in (pair_own, pair_far, pair_mask)]
    cross = call(
        cross_kernel, (n_day, 2 * part, mine_pairs), F32, 5, [pltpu.VMEM((width, n_sta * SLOTS), BF16)]
    )(*by_block, mine, got)
    summed = lax.all_to_all(cross, "day", split_axis=0, concat_axis=0, tiled=True).reshape(width, mine_pairs)
    scale = 1.0 / np.sqrt(width * n_day)
    high, low = lag_table(bins, n_day, scale)
    return call(stack_kernel, (mine_pairs, LAGS), F32, 3)(summed, jnp.asarray(high), jnp.asarray(low))


def solution(mesh):
    in_specs = (P("day", "sta", None), P("sta", None, None), P("sta"), P("sta"), P("sta"))
    out_specs = P(("sta", "day"), None)
    return jax.shard_map(local, mesh=mesh, in_specs=in_specs, out_specs=out_specs, check_vma=False)
```

time: 104 us -> 66.8 us (0.64)
  blocking collectives: 0 us -> 61.3 us
  waiting for transfers between devices: 52.5 us -> 0 us
  between operations: 13.5 us -> 0.06 us
  local copies, waits for them, and re-layouts: 13.1 us -> 0.87 us
  starting transfers between devices: 10.8 us -> 0 us
  other arithmetic: 10.6 us -> 0 us
  Pallas kernels: 0 us -> 3.5 us
  matrix products: 3.03 us -> 0 us
    all_to_all x0 -> x3, blocking collectives: none -> 61.3 us  [the longest x1 27.4 us: local(): lax.all_to_all(chosen, 'sta', split_axis=0, concat_axis=0, tiled=True)]
    reduce_scatter x1 -> x0, waiting for transfers between devices: 42.4 us -> none  [local(): summed = lax.psum_scatter(cross, 'day', scatter_dimension=0, tiled=True)]
    gather x3 -> x0, local copies, waits for them, and re-layouts: 12.1 us -> none  [the longest x1 5.08 us: local(): near = jnp.take(block, pair_own, axis=0).astype(jnp.float32)]
    all_to_all x1 -> x0, starting transfers between devices: 10.8 us -> none  [local(): lax.all_to_all(chosen, 'sta', split_axis=0, concat_axis=0, tiled=True)]
    all_to_all x1 -> x0, waiting for transfers between devices: 10 us -> none  [local(): lax.all_to_all(chosen, 'sta', split_axis=0, concat_axis=0, tiled=True)]
    cos x1 -> x0, other arithmetic: 4.18 us -> none  [lag_table(): return jnp.concatenate([jnp.cos(angle), -jnp.sin(angle)], axis=0)]
    pallas_call x0 -> x4, Pallas kernels: none -> 3.5 us  [the longest x1 1.57 us: local(): call(cross_kernel, (n_day, 2 * part, mine_pairs), F32, 5, [pltpu.VMEM((wi...]
    dot_general x1 -> x0, matrix products: 3.03 us -> none  [local(): jnp.dot(summed, table, precision=lax.Precision.HIGHEST, preferred_element...]
  transfers between devices with their start and end apart: 2 -> 0, of which waited for: 2 -> 0; matrix products, arithmetic and copies ran while one was open for 10% -> 0% of each run, Pallas kernels for 0% -> 0%
where the time goes in v1:
time: 66.8 us; the launch traced here: 65.7 us
  blocking collectives  61.3 us (92%)
  Pallas kernels  3.5 us (5%)
  local copies, waits for them, and re-layouts  0.87 us (1%)
    all_to_all x1, blocking collectives, local(): lax.all_to_all(chosen, 'sta', split_axis=0, concat_axis=0, tiled=True)  27.4 us
    all_to_all x1, blocking collectives, local(): lax.all_to_all(by_bin, 'day', split_axis=0, concat_axis=0, tiled=True)  18.5 us
    all_to_all x1, blocking collectives, local(): lax.all_to_all(cross, 'day', split_axis=0, concat_axis=0, tiled=True)  15.3 us
    pallas_call x1, Pallas kernels, local(): call(cross_kernel, (n_day, 2 * part, mine_pairs), F32, 5, [pltpu.VMEM((wi...  1.57 us
    pallas_call x1, Pallas kernels, local(): call(stack_kernel, (mine_pairs, LAGS), F32, 3)  1.43 us

profile of v1, /device:TPU:6, one launch (start us, length us, event | category | flops | bytes accessed | tf_op | source)
XLA Modules:
  0.0 65.7 jit_solution(5132625290815727418)
XLA Ops:
  0.0 0.0 copy-start.2
  0.0 0.8 %copy-done.2 = bf16[1,64,512]{2,1,0:T(8,128)(2,1)S(1)} copy-done((bf16[1,64,512]{2,1,0:T(8,128)(2,1)S(1)}, bf16[1,64,512]{2,1,0:T(8,128)(2,1)}, u32[]{:S(2)}) %copy-start.2) | copy-done | bytes 65560
  0.8 0.1 shard_map.73
  0.9 0.0 copy-start.3
  1.0 18.5 %all_to_all.15.mine_ref = bf16[8,32,128]{2,1,0:T(8,128)(2,1)S(1)} all-to-all(bf16[8,32,128]{2,1,0:T(8,128)(2,1)S(1)} %shard_map.73), channel_id=1, replica_groups=mesh['sta'=64,'day'=8] {'day'}, dimensions={0} | all-to-all | bytes 131072 | tf_op jit(solution)/shard_map/all_to_all | solution.py:108
  19.4 0.0 copy-done.3
  19.4 0.0 copy-start.4
  19.5 0.0 copy-start.5
  19.5 0.0 copy-start.6
  19.5 0.4 shard_map.74
  19.9 0.0 copy-start
  19.9 0.0 copy-start.1
  19.9 27.4 %all_to_all.16 = bf16[64,8,512]{2,1,0:T(8,128)(2,1)S(1)} all-to-all(bf16[64,8,512]{2,1,0:T(8,128)(2,1)S(1)} %shard_map.74), channel_id=1, replica_groups=mesh['sta'=64,'day'=8] {'sta'}, dimensions={0} | all-to-all | bytes 1048576 | tf_op jit(solution)/shard_map/all_to_all | solution.py:110
  47.3 0.0 copy-done.4
  47.3 0.0 copy-done.5
  47.3 0.0 copy-done.6
  47.4 1.6 %shard_map.75 = f32[8,64,128]{2,1,0:T(8,128)S(1)} custom-call(s32[8,128]{1,0:T(8,128)S(1)} %bitcast.11, s32[8,128]{1,0:T(8,128)S(1)} %bitcast.12, s32[8,128]{1,0:T(8,128)S(1)} %bitcast.13, bf16[8,32,128]{2,1,0:T(8,128)(2,1)S(1)} %all_to_all.15.mine_ref, bf16[512,512]{1,0:T(8,128)(2,1)S(1)} %bitcast.8), custom_call_target="tpu_custom_call" | custom-call | tf_op jit(solution)/shard_map/pallas_call | solution.py:112
  48.9 15.3 %all_to_all.17 = f32[8,64,128]{2,1,0:T(8,128)S(1)} all-to-all(f32[8,64,128]{2,1,0:T(8,128)S(1)} %shard_map.75), channel_id=1, replica_groups=mesh['sta'=64,'day'=8] {'day'}, dimensions={0} | all-to-all | bytes 524288 | tf_op jit(solution)/shard_map/all_to_all | solution.py:115
  64.3 0.0 copy-done
  64.3 0.0 copy-done.1
  64.3 1.4 %shard_map.76 = f32[128,1024]{1,0:T(8,128)} custom-call(f32[512,128]{1,0:T(8,128)S(1)} %bitcast.9, bf16[512,1024]{1,0:T(8,128)(2,1)S(1)} %copy-done.1, bf16[512,1024]{1,0:T(8,128)(2,1)S(1)} %copy-done), custom_call_target="tpu_custom_call" | custom-call | tf_op jit(solution)/shard_map/pallas_call | solution.py:118
Async XLA Ops:
  0.0 0.8 %copy-start.2 = (bf16[1,64,512]{2,1,0:T(8,128)(2,1)S(1)}, bf16[1,64,512]{2,1,0:T(8,128)(2,1)}, u32[]{:S(2)}) copy-start(bf16[1,64,512]{2,1,0:T(8,128)(2,1)} %x_ref.1) | copy-start | bytes 196612
  0.9 18.5 %copy-start.3 = (s32[1,64,8]{1,2,0:T(8,128)S(1)}, s32[1,64,8]{1,2,0:T(8,128)}, u32[]{:S(2)}) copy-start(s32[1,64,8]{1,2,0:T(8,128)} %param.8) | copy-start | bytes 6148
  19.4 27.9 %copy-start.4 = (s32[1024]{0:T(1024)S(1)}, s32[1024]{0:T(1024)}, u32[]{:S(2)}) copy-start(s32[1024]{0:T(1024)} %param.9) | copy-start | bytes 12292
  19.5 27.9 %copy-start.5 = (s32[1024]{0:T(1024)S(1)}, s32[1024]{0:T(1024)}, u32[]{:S(2)}) copy-start(s32[1024]{0:T(1024)} %param.10) | copy-start | bytes 12292
  19.5 27.9 %copy-start.6 = (s32[1024]{0:T(1024)S(1)}, s32[1024]{0:T(1024)}, u32[]{:S(2)}) copy-start(s32[1024]{0:T(1024)} %param.11) | copy-start | bytes 12292
  19.9 44.4 %copy-start = (bf16[512,1024]{1,0:T(8,128)(2,1)S(1)}, bf16[512,1024]{1,0:T(8,128)(2,1)}, u32[]{:S(2)}) copy-start(bf16[512,1024]{1,0:T(8,128)(2,1)} %constant.5.clone.low_ref) | copy-start | bytes 3145732
  19.9 44.4 %copy-start.1 = (bf16[512,1024]{1,0:T(8,128)(2,1)S(1)}, bf16[512,1024]{1,0:T(8,128)(2,1)}, u32[]{:S(2)}) copy-start(bf16[512,1024]{1,0:T(8,128)(2,1)} %constant.4.clone.high_ref) | copy-start | bytes 3145732

commit v2 on v1

v2 whole, which is shorter than its diff:
```python
import jax
import jax.numpy as jnp
import numpy as np
from jax import lax
from jax.experimental import pallas as pl
from jax.experimental.pallas import tpu as pltpu
from jax.sharding import PartitionSpec as P

SLOTS = 8
LAGS = 1024
BASE = 40
BF16 = jnp.bfloat16
F32 = jnp.float32
VMEM = pl.BlockSpec(memory_space=pltpu.VMEM)
HBM = pl.BlockSpec(memory_space=pltpu.HBM)


def lag_table(bins, n_day, scale):
    k = np.arange(bins)[:, None] + BASE
    m = np.arange(LAGS)[None, :] - LAGS // 2
    angle = 2.0 * np.pi / LAGS * (k * m % LAGS)
    part = bins // n_day
    both = np.stack([np.cos(angle), -np.sin(angle)]) * scale
    both = both.reshape(2, n_day, part, LAGS).transpose(1, 0, 2, 3).reshape(2 * bins, LAGS).astype(np.float32)
    high = both.astype(jnp.bfloat16)
    low = (both - high.astype(np.float32)).astype(jnp.bfloat16)
    return high, low


def turn_kernel(x_ref, out_ref):
    n_day, part, _ = out_ref.shape
    bins = n_day * part
    x = x_ref[0].astype(F32)
    y = jnp.concatenate([x[:, :bins], x[:, bins:]], axis=0)
    out_ref[...] = y.T.astype(BF16).reshape(out_ref.shape)


def pick_kernel(picks_ref, mine_ref, out_ref):
    slots, owners = picks_ref.shape
    n_day, part, twice = mine_ref.shape
    rows = n_day * part
    mine = mine_ref[...].reshape(rows, twice)
    picks = picks_ref[...]
    lane = lax.broadcasted_iota(jnp.int32, (slots, twice), 1)
    for half in range(2):
        hot = jnp.concatenate(
            [(lane == picks[:, o : o + 1] + half * (twice // 2)).astype(F32) for o in range(owners)], axis=0
        ).astype(BF16)
        got = lax.dot_general(hot, mine, (((1,), (1,)), ((), ())), preferred_element_type=F32)
        out_ref[:, :, half * rows : (half + 1) * rows] = got.astype(BF16).reshape(owners, slots, rows)


def cross_kernel(own_ref, far_ref, mask_ref, mine_ref, got_ref, out_ref, turned):
    n_day, part, twice = mine_ref.shape
    rows = n_day * part
    blocks, lanes = own_ref.shape
    mine = mine_ref[...].reshape(rows, twice)
    turned[...] = got_ref[...].T
    near_row = lax.broadcasted_iota(jnp.int32, (twice, 2 * lanes), 0)
    far_row = lax.broadcasted_iota(jnp.int32, (got_ref.shape[0], 2 * lanes), 0)
    for j in range(0, blocks, 2):
        own = jnp.where(mask_ref[j : j + 2, :] > 0, own_ref[j : j + 2, :], 2 * twice)
        own = jnp.concatenate([own[:1], own[1:]], axis=1)
        far = jnp.concatenate([far_ref[j : j + 1, :], far_ref[j + 1 : j + 2, :]], axis=1)
        hot_far = (far_row == far).astype(F32).astype(BF16)
        hot_re = (near_row == own).astype(F32).astype(BF16)
        hot_im = (near_row == own + twice // 2).astype(F32).astype(BF16)
        near_re = jnp.dot(mine, hot_re, preferred_element_type=F32)
        near_im = jnp.dot(mine, hot_im, preferred_element_type=F32)
        both = jnp.dot(turned[...], hot_far, preferred_element_type=F32)
        far_re, far_im = both[:rows], both[rows:]
        real = jnp.sum((near_re * far_re + near_im * far_im).reshape(n_day, part, 2 * lanes), axis=0)
        imag = jnp.sum((near_im * far_re - near_re * far_im).reshape(n_day, part, 2 * lanes), axis=0)
        for i in range(2):
            out_ref[j + i, :part, :] = real[:, i * lanes : (i + 1) * lanes]
            out_ref[j + i, part:, :] = imag[:, i * lanes : (i + 1) * lanes]


def stack_kernel(summed_ref, high_ref, low_ref, out_hbm, stage, sems):
    rows, lags = stage.shape
    turned = summed_ref[...].T
    high = turned.astype(BF16)
    low = (turned - high.astype(F32)).astype(BF16)
    both = jnp.concatenate([high, low], axis=0)
    step = lags // 2
    copies = []
    for j in range(2):
        at = slice(j * step, (j + 1) * step)
        out = jnp.dot(both, high_ref[:, at], preferred_element_type=F32)
        stage[:, at] = out[:rows] + out[rows:] + jnp.dot(high, low_ref[:, at], preferred_element_type=F32)
        copies.append(pltpu.make_async_copy(stage.at[:, at], out_hbm.at[:, at], sems.at[j]))
        copies[j].start()
    for copy in copies:
        copy.wait()


def call(kernel, out_shape, in_specs, out_specs, scratch=()):
    return pl.pallas_call(
        kernel,
        out_shape=out_shape,
        in_specs=in_specs,
        out_specs=out_specs,
        scratch_shapes=list(scratch),
        compiler_params=pltpu.CompilerParams(vmem_limit_bytes=48 * 1024 * 1024),
    )


def local(spectra, picks, pair_own, pair_far, pair_mask):
    n_sta = lax.axis_size("sta")
    n_day = lax.axis_size("day")
    _, stations, width = spectra.shape
    bins = width // 2
    part = bins // n_day
    pairs = pair_own.shape[0]
    mine_pairs = pairs // n_day
    slots = n_sta * SLOTS
    shape = jax.ShapeDtypeStruct
    dma = pltpu.SemaphoreType.DMA
    own, far, mask = [a.reshape(n_day, mine_pairs) for a in (pair_own, pair_far, pair_mask)]

    by_bin = call(turn_kernel, shape((n_day, part, 2 * stations), BF16), [VMEM], VMEM)(spectra)
    mine = lax.all_to_all(by_bin, "day", split_axis=0, concat_axis=0, tiled=True)
    chosen = call(pick_kernel, shape((n_sta, SLOTS, width), BF16), [VMEM] * 2, VMEM)(picks[0].T, mine)
    got = lax.all_to_all(chosen, "sta", split_axis=0, concat_axis=0, tiled=True).reshape(slots, width)
    cross = call(
        cross_kernel,
        shape((n_day, 2 * part, mine_pairs), F32),
        [VMEM] * 5,
        VMEM,
        [pltpu.VMEM((width, slots), BF16)],
    )(own, far, mask, mine, got)
    summed = lax.all_to_all(cross, "day", split_axis=0, concat_axis=0, tiled=True).reshape(width, mine_pairs)
    high, low = lag_table(bins, n_day, 1.0 / np.sqrt(width * n_day))
    return call(
        stack_kernel,
        shape((mine_pairs, LAGS), F32),
        [VMEM] * 3,
        HBM,
        [pltpu.VMEM((mine_pairs, LAGS), F32), dma((2,))],
    )(summed, jnp.asarray(high), jnp.asarray(low))


def solution(mesh):
    in_specs = (P("day", "sta", None), P("sta", None, None), P("sta"), P("sta"), P("sta"))
    out_specs = P(("sta", "day"), None)
    return jax.shard_map(local, mesh=mesh, in_specs=in_specs, out_specs=out_specs, check_vma=False)
```

time: 66.8 us -> 66.3 us (level)
  no operation moved by 1% of the time
where the time goes in v2:
time: 66.3 us; the launch traced here: 65.2 us
  blocking collectives  61.3 us (92%)
  Pallas kernels  2.99 us (5%)
  local copies, waits for them, and re-layouts  0.87 us (1%)
    all_to_all x1, blocking collectives, local(): lax.all_to_all(chosen, 'sta', split_axis=0, concat_axis=0, tiled=True)  27.4 us
    all_to_all x1, blocking collectives, local(): lax.all_to_all(by_bin, 'day', split_axis=0, concat_axis=0, tiled=True)  18.5 us
    all_to_all x1, blocking collectives, local(): lax.all_to_all(cross, 'day', split_axis=0, concat_axis=0, tiled=True)  15.3 us
    pallas_call x1, Pallas kernels, local(): call(stack_kernel, shape((mine_pairs, LAGS), F32), [VMEM] * 3, HBM, [pltp...  1.34 us

profile of v2, /device:TPU:6, one launch (start us, length us, event | category | flops | bytes accessed | tf_op | source)
XLA Modules:
  0.0 65.2 jit_solution(10465547220987768302)
XLA Ops:
  0.0 0.0 copy-start.2
  0.0 0.8 %copy-done.2 = bf16[1,64,512]{2,1,0:T(8,128)(2,1)S(1)} copy-done((bf16[1,64,512]{2,1,0:T(8,128)(2,1)S(1)}, bf16[1,64,512]{2,1,0:T(8,128)(2,1)}, u32[]{:S(2)}) %copy-start.2) | copy-done | bytes 65560
  0.8 0.1 shard_map.73
  0.9 0.0 copy-start.3
  1.0 18.5 %all_to_all.15.mine_ref = bf16[8,32,128]{2,1,0:T(8,128)(2,1)S(1)} all-to-all(bf16[8,32,128]{2,1,0:T(8,128)(2,1)S(1)} %shard_map.73), channel_id=1, replica_groups=mesh['sta'=64,'day'=8] {'day'}, dimensions={0} | all-to-all | bytes 131072 | tf_op jit(solution)/shard_map/all_to_all | solution.py:122
  19.4 0.0 copy-done.3
  19.4 0.0 copy-start.4
  19.5 0.0 copy-start.5
  19.5 0.0 copy-start.6
  19.5 0.4 shard_map.74
  19.9 0.0 copy-start
  19.9 0.0 copy-start.1
  19.9 27.4 %all_to_all.16 = bf16[64,8,512]{2,1,0:T(8,128)(2,1)S(1)} all-to-all(bf16[64,8,512]{2,1,0:T(8,128)(2,1)S(1)} %shard_map.74), channel_id=1, replica_groups=mesh['sta'=64,'day'=8] {'sta'}, dimensions={0} | all-to-all | bytes 1048576 | tf_op jit(solution)/shard_map/all_to_all | solution.py:124
  47.3 0.0 copy-done.4
  47.3 0.0 copy-done.5
  47.3 0.0 copy-done.6
  47.4 1.1 %shard_map.75 = f32[8,64,128]{2,1,0:T(8,128)S(1)} custom-call(s32[8,128]{1,0:T(8,128)S(1)} %bitcast.11, s32[8,128]{1,0:T(8,128)S(1)} %bitcast.12, s32[8,128]{1,0:T(8,128)S(1)} %bitcast.13, bf16[8,32,128]{2,1,0:T(8,128)(2,1)S(1)} %all_to_all.15.mine_ref, bf16[512,512]{1,0:T(8,128)(2,1)S(1)} %bitcast.8), custom_call_target="tpu_custom_call" | custom-call | tf_op jit(solution)/shard_map/pallas_call | solution.py:125
  48.5 15.3 %all_to_all.17 = f32[8,64,128]{2,1,0:T(8,128)S(1)} all-to-all(f32[8,64,128]{2,1,0:T(8,128)S(1)} %shard_map.75), channel_id=1, replica_groups=mesh['sta'=64,'day'=8] {'day'}, dimensions={0} | all-to-all | bytes 524288 | tf_op jit(solution)/shard_map/all_to_all | solution.py:132
  63.8 0.0 copy-done
  63.9 0.0 copy-done.1
  63.9 1.3 %shard_map.76 = f32[128,1024]{1,0:T(8,128)} custom-call(f32[512,128]{1,0:T(8,128)S(1)} %bitcast.9, bf16[512,1024]{1,0:T(8,128)(2,1)S(1)} %copy-done.1, bf16[512,1024]{1,0:T(8,128)(2,1)S(1)} %copy-done), custom_call_target="tpu_custom_call" | custom-call | tf_op jit(solution)/shard_map/pallas_call | solution.py:134
Async XLA Ops:
  0.0 0.8 %copy-start.2 = (bf16[1,64,512]{2,1,0:T(8,128)(2,1)S(1)}, bf16[1,64,512]{2,1,0:T(8,128)(2,1)}, u32[]{:S(2)}) copy-start(bf16[1,64,512]{2,1,0:T(8,128)(2,1)} %x_ref.1) | copy-start | bytes 196612
  0.9 18.5 %copy-start.3 = (s32[1,64,8]{1,2,0:T(8,128)S(1)}, s32[1,64,8]{1,2,0:T(8,128)}, u32[]{:S(2)}) copy-start(s32[1,64,8]{1,2,0:T(8,128)} %param.8) | copy-start | bytes 6148
  19.4 27.9 %copy-start.4 = (s32[1024]{0:T(1024)S(1)}, s32[1024]{0:T(1024)}, u32[]{:S(2)}) copy-start(s32[1024]{0:T(1024)} %param.9) | copy-start | bytes 12292
  19.5 27.9 %copy-start.5 = (s32[1024]{0:T(1024)S(1)}, s32[1024]{0:T(1024)}, u32[]{:S(2)}) copy-start(s32[1024]{0:T(1024)} %param.10) | copy-start | bytes 12292
  19.5 27.9 %copy-start.6 = (s32[1024]{0:T(1024)S(1)}, s32[1024]{0:T(1024)}, u32[]{:S(2)}) copy-start(s32[1024]{0:T(1024)} %param.11) | copy-start | bytes 12292
  19.9 44.0 %copy-start = (bf16[512,1024]{1,0:T(8,128)(2,1)S(1)}, bf16[512,1024]{1,0:T(8,128)(2,1)}, u32[]{:S(2)}) copy-start(bf16[512,1024]{1,0:T(8,128)(2,1)} %constant.5.clone.low_ref) | copy-start | bytes 3145732
  19.9 44.0 %copy-start.1 = (bf16[512,1024]{1,0:T(8,128)(2,1)S(1)}, bf16[512,1024]{1,0:T(8,128)(2,1)}, u32[]{:S(2)}) copy-start(bf16[512,1024]{1,0:T(8,128)(2,1)} %constant.4.clone.high_ref) | copy-start | bytes 3145732

commit v3 on v2

--- a/solution.py
+++ b/solution.py
@@ -38,16 +38,14 @@
 def pick_kernel(picks_ref, mine_ref, out_ref):
     slots, owners = picks_ref.shape
     n_day, part, twice = mine_ref.shape
-    rows = n_day * part
-    mine = mine_ref[...].reshape(rows, twice)
+    stations = twice // 2
+    turned = mine_ref[...].reshape(n_day * part, twice).T
+    source = jnp.concatenate([turned[:stations], turned[stations:]], axis=1)
     picks = picks_ref[...]
-    lane = lax.broadcasted_iota(jnp.int32, (slots, twice), 1)
-    for half in range(2):
-        hot = jnp.concatenate(
-            [(lane == picks[:, o : o + 1] + half * (twice // 2)).astype(F32) for o in range(owners)], axis=0
-        ).astype(BF16)
-        got = lax.dot_general(hot, mine, (((1,), (1,)), ((), ())), preferred_element_type=F32)
-        out_ref[:, :, half * rows : (half + 1) * rows] = got.astype(BF16).reshape(owners, slots, rows)
+    lane = lax.broadcasted_iota(jnp.int32, (slots, stations), 1)
+    hot = jnp.concatenate([(lane == picks[:, o : o + 1]).astype(F32) for o in range(owners)], axis=0).astype(BF16)
+    got = jnp.dot(hot, source, preferred_element_type=F32)
+    out_ref[...] = got.astype(BF16).reshape(out_ref.shape)
 
 
 def cross_kernel(own_ref, far_ref, mask_ref, mine_ref, got_ref, out_ref, turned):
@@ -63,11 +61,11 @@
         own = jnp.concatenate([own[:1], own[1:]], axis=1)
         far = jnp.concatenate([far_ref[j : j + 1, :], far_ref[j + 1 : j + 2, :]], axis=1)
         hot_far = (far_row == far).astype(F32).astype(BF16)
+        both = jnp.dot(turned[...], hot_far, preferred_element_type=F32)
         hot_re = (near_row == own).astype(F32).astype(BF16)
         hot_im = (near_row == own + twice // 2).astype(F32).astype(BF16)
         near_re = jnp.dot(mine, hot_re, preferred_element_type=F32)
         near_im = jnp.dot(mine, hot_im, preferred_element_type=F32)
-        both = jnp.dot(turned[...], hot_far, preferred_element_type=F32)
         far_re, far_im = both[:rows], both[rows:]
         real = jnp.sum((near_re * far_re + near_im * far_im).reshape(n_day, part, 2 * lanes), axis=0)
         imag = jnp.sum((near_im * far_re - near_re * far_im).reshape(n_day, part, 2 * lanes), axis=0)

time: 66.3 us -> 66.1 us (level)
  no operation moved by 1% of the time
where the time goes in v3:
time: 66.1 us; the launch traced here: 65 us
  blocking collectives  61.3 us (93%)
  Pallas kernels  2.82 us (4%)
  local copies, waits for them, and re-layouts  0.87 us (1%)
    all_to_all x1, blocking collectives, local(): lax.all_to_all(chosen, 'sta', split_axis=0, concat_axis=0, tiled=True)  27.4 us
    all_to_all x1, blocking collectives, local(): lax.all_to_all(by_bin, 'day', split_axis=0, concat_axis=0, tiled=True)  18.5 us
    all_to_all x1, blocking collectives, local(): lax.all_to_all(cross, 'day', split_axis=0, concat_axis=0, tiled=True)  15.3 us
    pallas_call x1, Pallas kernels, local(): call(stack_kernel, shape((mine_pairs, LAGS), F32), [VMEM] * 3, HBM, [pltp...  1.34 us

profile of v3, /device:TPU:6, one launch (start us, length us, event | category | flops | bytes accessed | tf_op | source)
XLA Modules:
  0.0 65.0 jit_solution(583845212258831055)
XLA Ops:
  0.0 0.0 copy-start.2
  0.0 0.8 %copy-done.2 = bf16[1,64,512]{2,1,0:T(8,128)(2,1)S(1)} copy-done((bf16[1,64,512]{2,1,0:T(8,128)(2,1)S(1)}, bf16[1,64,512]{2,1,0:T(8,128)(2,1)}, u32[]{:S(2)}) %copy-start.2) | copy-done | bytes 65560
  0.8 0.1 shard_map.73
  0.9 0.0 copy-start.3
  1.0 18.5 %all_to_all.15.mine_ref = bf16[8,32,128]{2,1,0:T(8,128)(2,1)S(1)} all-to-all(bf16[8,32,128]{2,1,0:T(8,128)(2,1)S(1)} %shard_map.73), channel_id=1, replica_groups=mesh['sta'=64,'day'=8] {'day'}, dimensions={0} | all-to-all | bytes 131072 | tf_op jit(solution)/shard_map/all_to_all | solution.py:120
  19.4 0.0 copy-done.3
  19.4 0.0 copy-start.4
  19.5 0.0 copy-start.5
  19.5 0.0 copy-start.6
  19.5 0.4 shard_map.74
  19.8 0.0 copy-start
  19.8 0.0 copy-start.1
  19.8 27.4 %all_to_all.16 = bf16[64,8,512]{2,1,0:T(8,128)(2,1)S(1)} all-to-all(bf16[64,8,512]{2,1,0:T(8,128)(2,1)S(1)} %shard_map.74), channel_id=1, replica_groups=mesh['sta'=64,'day'=8] {'sta'}, dimensions={0} | all-to-all | bytes 1048576 | tf_op jit(solution)/shard_map/all_to_all | solution.py:122
  47.3 0.0 copy-done.4
  47.3 0.0 copy-done.5
  47.3 0.0 copy-done.6
  47.3 1.0 %shard_map.75 = f32[8,64,128]{2,1,0:T(8,128)S(1)} custom-call(s32[8,128]{1,0:T(8,128)S(1)} %bitcast.11, s32[8,128]{1,0:T(8,128)S(1)} %bitcast.12, s32[8,128]{1,0:T(8,128)S(1)} %bitcast.13, bf16[8,32,128]{2,1,0:T(8,128)(2,1)S(1)} %all_to_all.15.mine_ref, bf16[512,512]{1,0:T(8,128)(2,1)S(1)} %bitcast.8), custom_call_target="tpu_custom_call" | custom-call | tf_op jit(solution)/shard_map/pallas_call | solution.py:123
  48.3 15.3 %all_to_all.17 = f32[8,64,128]{2,1,0:T(8,128)S(1)} all-to-all(f32[8,64,128]{2,1,0:T(8,128)S(1)} %shard_map.75), channel_id=1, replica_groups=mesh['sta'=64,'day'=8] {'day'}, dimensions={0} | all-to-all | bytes 524288 | tf_op jit(solution)/shard_map/all_to_all | solution.py:130
  63.7 0.0 copy-done
  63.7 0.0 copy-done.1
  63.7 1.3 %shard_map.76 = f32[128,1024]{1,0:T(8,128)} custom-call(f32[512,128]{1,0:T(8,128)S(1)} %bitcast.9, bf16[512,1024]{1,0:T(8,128)(2,1)S(1)} %copy-done.1, bf16[512,1024]{1,0:T(8,128)(2,1)S(1)} %copy-done), custom_call_target="tpu_custom_call" | custom-call | tf_op jit(solution)/shard_map/pallas_call | solution.py:132
Async XLA Ops:
  0.0 0.8 %copy-start.2 = (bf16[1,64,512]{2,1,0:T(8,128)(2,1)S(1)}, bf16[1,64,512]{2,1,0:T(8,128)(2,1)}, u32[]{:S(2)}) copy-start(bf16[1,64,512]{2,1,0:T(8,128)(2,1)} %x_ref.1) | copy-start | bytes 196612
  0.9 18.5 %copy-start.3 = (s32[1,64,8]{1,2,0:T(8,128)S(1)}, s32[1,64,8]{1,2,0:T(8,128)}, u32[]{:S(2)}) copy-start(s32[1,64,8]{1,2,0:T(8,128)} %param.8) | copy-start | bytes 6148
  19.4 27.8 %copy-start.4 = (s32[1024]{0:T(1024)S(1)}, s32[1024]{0:T(1024)}, u32[]{:S(2)}) copy-start(s32[1024]{0:T(1024)} %param.9) | copy-start | bytes 12292
  19.5 27.8 %copy-start.5 = (s32[1024]{0:T(1024)S(1)}, s32[1024]{0:T(1024)}, u32[]{:S(2)}) copy-start(s32[1024]{0:T(1024)} %param.10) | copy-start | bytes 12292
  19.5 27.8 %copy-start.6 = (s32[1024]{0:T(1024)S(1)}, s32[1024]{0:T(1024)}, u32[]{:S(2)}) copy-start(s32[1024]{0:T(1024)} %param.11) | copy-start | bytes 12292
  19.8 43.9 %copy-start = (bf16[512,1024]{1,0:T(8,128)(2,1)S(1)}, bf16[512,1024]{1,0:T(8,128)(2,1)}, u32[]{:S(2)}) copy-start(bf16[512,1024]{1,0:T(8,128)(2,1)} %constant.5.clone.low_ref) | copy-start | bytes 3145732
  19.8 43.9 %copy-start.1 = (bf16[512,1024]{1,0:T(8,128)(2,1)S(1)}, bf16[512,1024]{1,0:T(8,128)(2,1)}, u32[]{:S(2)}) copy-start(bf16[512,1024]{1,0:T(8,128)(2,1)} %constant.4.clone.high_ref) | copy-start | bytes 3145732

commit v4 on v3

--- a/solution.py
+++ b/solution.py
@@ -16,23 +16,36 @@
 
 
 def lag_table(bins, n_day, scale):
-    k = np.arange(bins)[:, None] + BASE
-    m = np.arange(LAGS)[None, :] - LAGS // 2
+    k = np.concatenate([np.arange(0, bins, 2), np.arange(1, bins, 2)])[:, None] + BASE
+    m = np.arange(LAGS // 2)[None, :] - LAGS // 2
     angle = 2.0 * np.pi / LAGS * (k * m % LAGS)
     part = bins // n_day
     both = np.stack([np.cos(angle), -np.sin(angle)]) * scale
-    both = both.reshape(2, n_day, part, LAGS).transpose(1, 0, 2, 3).reshape(2 * bins, LAGS).astype(np.float32)
+    both = both.reshape(2, n_day, part, -1).transpose(1, 0, 2, 3).reshape(2 * bins, -1).astype(np.float32)
     high = both.astype(jnp.bfloat16)
     low = (both - high.astype(np.float32)).astype(jnp.bfloat16)
     return high, low
 
 
-def turn_kernel(x_ref, out_ref):
-    n_day, part, _ = out_ref.shape
-    bins = n_day * part
+def open_kernel(x_hbm, picks_hbm, own_hbm, mask_hbm, far_hbm, by_bin_ref, picks_ref, row_ref, far_ref, *scratch):
+    x_ref, own_ref, mask_ref, turned, sems = scratch
+    copies = [
+        pltpu.make_async_copy(source, target, sems.at[i])
+        for i, (source, target) in enumerate(
+            [(x_hbm, x_ref), (picks_hbm, picks_ref), (own_hbm, own_ref), (mask_hbm, mask_ref), (far_hbm, far_ref)]
+        )
+    ]
+    for copy in copies:
+        copy.start()
+    bins, twice = turned.shape
+    for copy in copies[1:]:
+        copy.wait()
+    row_ref[...] = jnp.where(mask_ref[...] > 0, own_ref[...], 2 * twice)
+    copies[0].wait()
     x = x_ref[0].astype(F32)
-    y = jnp.concatenate([x[:, :bins], x[:, bins:]], axis=0)
-    out_ref[...] = y.T.astype(BF16).reshape(out_ref.shape)
+    turned[...] = jnp.concatenate([x[:, :bins], x[:, bins:]], axis=0).T
+    by_parity = [turned[pl.ds(odd, bins // 2, stride=2), :] for odd in range(2)]
+    by_bin_ref[...] = jnp.concatenate(by_parity, axis=0).astype(BF16).reshape(by_bin_ref.shape)
 
 
 def pick_kernel(picks_ref, mine_ref, out_ref):
@@ -48,7 +61,7 @@
     out_ref[...] = got.astype(BF16).reshape(out_ref.shape)
 
 
-def cross_kernel(own_ref, far_ref, mask_ref, mine_ref, got_ref, out_ref, turned):
+def cross_kernel(own_ref, far_ref, mine_ref, got_ref, out_ref, turned):
     n_day, part, twice = mine_ref.shape
     rows = n_day * part
     blocks, lanes = own_ref.shape
@@ -57,8 +70,7 @@
     near_row = lax.broadcasted_iota(jnp.int32, (twice, 2 * lanes), 0)
     far_row = lax.broadcasted_iota(jnp.int32, (got_ref.shape[0], 2 * lanes), 0)
     for j in range(0, blocks, 2):
-        own = jnp.where(mask_ref[j : j + 2, :] > 0, own_ref[j : j + 2, :], 2 * twice)
-        own = jnp.concatenate([own[:1], own[1:]], axis=1)
+        own = jnp.concatenate([own_ref[j : j + 1, :], own_ref[j + 1 : j + 2, :]], axis=1)
         far = jnp.concatenate([far_ref[j : j + 1, :], far_ref[j + 1 : j + 2, :]], axis=1)
         hot_far = (far_row == far).astype(F32).astype(BF16)
         both = jnp.dot(turned[...], hot_far, preferred_element_type=F32)
@@ -80,14 +92,22 @@
     high = turned.astype(BF16)
     low = (turned - high.astype(F32)).astype(BF16)
     both = jnp.concatenate([high, low], axis=0)
-    step = lags // 2
+    depth = both.shape[1] // 2
+    step = lags // 4
     copies = []
     for j in range(2):
         at = slice(j * step, (j + 1) * step)
-        out = jnp.dot(both, high_ref[:, at], preferred_element_type=F32)
-        stage[:, at] = out[:rows] + out[rows:] + jnp.dot(high, low_ref[:, at], preferred_element_type=F32)
-        copies.append(pltpu.make_async_copy(stage.at[:, at], out_hbm.at[:, at], sems.at[j]))
-        copies[j].start()
+        sums = []
+        for odd in range(2):
+            bins = slice(odd * depth, (odd + 1) * depth)
+            out = jnp.dot(both[:, bins], high_ref[bins, at], preferred_element_type=F32)
+            out_low = jnp.dot(high[:, bins], low_ref[bins, at], preferred_element_type=F32)
+            sums.append(out[:rows] + out[rows:] + out_low)
+        for half, total in enumerate((sums[0] + sums[1], sums[0] - sums[1])):
+            to = slice(half * lags // 2 + j * step, half * lags // 2 + (j + 1) * step)
+            stage[:, to] = total
+            copies.append(pltpu.make_async_copy(stage.at[:, to], out_hbm.at[:, to], sems.at[2 * j + half]))
+            copies[-1].start()
     for copy in copies:
         copy.wait()
 
@@ -116,17 +136,29 @@
     dma = pltpu.SemaphoreType.DMA
     own, far, mask = [a.reshape(n_day, mine_pairs) for a in (pair_own, pair_far, pair_mask)]
 
-    by_bin = call(turn_kernel, shape((n_day, part, 2 * stations), BF16), [VMEM], VMEM)(spectra)
+    given = [pltpu.with_memory_space_constraint(a, pltpu.HBM) for a in (spectra, picks[0].T, own, mask, far)]
+    by_bin, picks, rows, far = call(
+        open_kernel,
+        (
+            shape((n_day, part, 2 * stations), BF16),
+            shape((SLOTS, n_sta), jnp.int32),
+            shape((n_day, mine_pairs), jnp.int32),
+            shape((n_day, mine_pairs), jnp.int32),
+        ),
+        [HBM] * 5,
+        (VMEM,) * 4,
+        [pltpu.VMEM(a.shape, a.dtype) for a in (spectra, own, mask)] + [pltpu.VMEM((bins, 2 * stations), F32), dma((5,))],
+    )(*given)
     mine = lax.all_to_all(by_bin, "day", split_axis=0, concat_axis=0, tiled=True)
-    chosen = call(pick_kernel, shape((n_sta, SLOTS, width), BF16), [VMEM] * 2, VMEM)(picks[0].T, mine)
+    chosen = call(pick_kernel, shape((n_sta, SLOTS, width), BF16), [VMEM] * 2, VMEM)(picks, mine)
     got = lax.all_to_all(chosen, "sta", split_axis=0, concat_axis=0, tiled=True).reshape(slots, width)
     cross = call(
         cross_kernel,
         shape((n_day, 2 * part, mine_pairs), F32),
-        [VMEM] * 5,
+        [VMEM] * 4,
         VMEM,
         [pltpu.VMEM((width, slots), BF16)],
-    )(own, far, mask, mine, got)
+    )(rows, far, mine, got)
     summed = lax.all_to_all(cross, "day", split_axis=0, concat_axis=0, tiled=True).reshape(width, mine_pairs)
     high, low = lag_table(bins, n_day, 1.0 / np.sqrt(width * n_day))
     return call(
@@ -134,7 +166,7 @@
         shape((mine_pairs, LAGS), F32),
         [VMEM] * 3,
         HBM,
-        [pltpu.VMEM((mine_pairs, LAGS), F32), dma((2,))],
+        [pltpu.VMEM((mine_pairs, LAGS), F32), dma((4,))],
     )(summed, jnp.asarray(high), jnp.asarray(low))
 
 

time: 66.1 us -> 65.8 us (level)
  local copies, waits for them, and re-layouts: 0.87 us -> 0.01 us
  Pallas kernels: 2.82 us -> 3.56 us
    pallas_call x2, Pallas kernels: 1.13 us -> 2.03 us  [the longest x1 1.02 us: local(): call(cross_kernel, shape((n_day, 2 * part, mine_pairs), F32), [VMEM] * 4,...]
    unnamed x14 -> x4, local copies, waits for them, and re-layouts: 0.87 us -> 0.01 us
where the time goes in v4:
time: 65.8 us; the launch traced here: 64.7 us
  blocking collectives  61.1 us (93%)
  Pallas kernels  3.56 us (5%)
    all_to_all x1, blocking collectives, local(): lax.all_to_all(chosen, 'sta', split_axis=0, concat_axis=0, tiled=True)  27.3 us
    all_to_all x1, blocking collectives, local(): lax.all_to_all(by_bin, 'day', split_axis=0, concat_axis=0, tiled=True)  18.5 us
    all_to_all x1, blocking collectives, local(): lax.all_to_all(cross, 'day', split_axis=0, concat_axis=0, tiled=True)  15.3 us

profile of v4, /device:TPU:6, one launch (start us, length us, event | category | flops | bytes accessed | tf_op | source)
XLA Modules:
  0.0 64.7 jit_solution(1448085418009326523)
XLA Ops:
  0.0 1.0 %shard_map.73 = (bf16[8,32,128]{2,1,0:T(8,128)(2,1)S(1)}, s32[8,64]{1,0:T(8,128)S(1)}, s32[8,128]{1,0:T(8,128)S(1)}, s32[8,128]{1,0:T(8,128)S(1)}) custom-call(bf16[1,64,512]{2,1,0:T(8,128)(2,1)} %x_hbm.1, s32[8,64]{1,0:T(8,128)} %bitcast.10, s32[8,128]{1,0:T(8,128)} %bitcast.11, s32[8,128]{1,0:T(8,128)} %bitcast.12, s32[8,128]{1,0:T(8,128)} %bitcast.13), custom_call_target="tpu_custom_call" | custom-call | tf_op jit(solution)/shard_map/pallas_call | solution.py:140
  1.0 18.5 %all_to_all.15.mine_ref = bf16[8,32,128]{2,1,0:T(8,128)(2,1)S(1)} all-to-all(bf16[8,32,128]{2,1,0:T(8,128)(2,1)S(1)} %get-tuple-element.11), channel_id=1, replica_groups=mesh['sta'=64,'day'=8] {'day'}, dimensions={0} | all-to-all | bytes 131072 | tf_op jit(solution)/shard_map/all_to_all | solution.py:152
  19.5 0.4 shard_map.74
  19.9 27.3 %all_to_all.16 = bf16[64,8,512]{2,1,0:T(8,128)(2,1)S(1)} all-to-all(bf16[64,8,512]{2,1,0:T(8,128)(2,1)S(1)} %shard_map.74), channel_id=1, replica_groups=mesh['sta'=64,'day'=8] {'sta'}, dimensions={0} | all-to-all | bytes 1048576 | tf_op jit(solution)/shard_map/all_to_all | solution.py:154
  47.2 0.0 copy-start
  47.2 0.0 copy-start.1
  47.2 1.0 %shard_map.75 = f32[8,64,128]{2,1,0:T(8,128)S(1)} custom-call(s32[8,128]{1,0:T(8,128)S(1)} %get-tuple-element.9.own_ref, s32[8,128]{1,0:T(8,128)S(1)} %get-tuple-element.10.far_ref, bf16[8,32,128]{2,1,0:T(8,128)(2,1)S(1)} %all_to_all.15.mine_ref, bf16[512,512]{1,0:T(8,128)(2,1)S(1)} %bitcast.8), custom_call_target="tpu_custom_call" | custom-call | tf_op jit(solution)/shard_map/pallas_call | solution.py:155
  48.2 15.3 %all_to_all.17 = f32[8,64,128]{2,1,0:T(8,128)S(1)} all-to-all(f32[8,64,128]{2,1,0:T(8,128)S(1)} %shard_map.75), channel_id=1, replica_groups=mesh['sta'=64,'day'=8] {'day'}, dimensions={0} | all-to-all | bytes 524288 | tf_op jit(solution)/shard_map/all_to_all | solution.py:162
  63.5 0.0 copy-done
  63.5 0.0 copy-done.1
  63.5 1.2 %shard_map.76 = f32[128,1024]{1,0:T(8,128)} custom-call(f32[512,128]{1,0:T(8,128)S(1)} %bitcast.9, bf16[512,512]{1,0:T(8,128)(2,1)S(1)} %copy-done.1, bf16[512,512]{1,0:T(8,128)(2,1)S(1)} %copy-done), custom_call_target="tpu_custom_call" | custom-call | tf_op jit(solution)/shard_map/pallas_call | solution.py:164
Async XLA Ops:
  47.2 16.4 %copy-start = (bf16[512,512]{1,0:T(8,128)(2,1)S(1)}, bf16[512,512]{1,0:T(8,128)(2,1)}, u32[]{:S(2)}) copy-start(bf16[512,512]{1,0:T(8,128)(2,1)} %constant.5.clone.low_ref) | copy-start | bytes 1572868
  47.2 16.4 %copy-start.1 = (bf16[512,512]{1,0:T(8,128)(2,1)S(1)}, bf16[512,512]{1,0:T(8,128)(2,1)}, u32[]{:S(2)}) copy-start(bf16[512,512]{1,0:T(8,128)(2,1)} %constant.4.clone.high_ref) | copy-start | bytes 1572868

commit v5 on v4

--- a/solution.py
+++ b/solution.py
@@ -9,6 +9,7 @@
 SLOTS = 8
 LAGS = 1024
 BASE = 40
+PIECES = 2
 BF16 = jnp.bfloat16
 F32 = jnp.float32
 VMEM = pl.BlockSpec(memory_space=pltpu.VMEM)
@@ -29,19 +30,23 @@
 
 def open_kernel(x_hbm, picks_hbm, own_hbm, mask_hbm, far_hbm, by_bin_ref, picks_ref, row_ref, far_ref, *scratch):
     x_ref, own_ref, mask_ref, turned, sems = scratch
+    step = x_ref.shape[1] // PIECES
+    pieces = [pl.ds(i * step, step) for i in range(PIECES)]
     copies = [
         pltpu.make_async_copy(source, target, sems.at[i])
         for i, (source, target) in enumerate(
-            [(x_hbm, x_ref), (picks_hbm, picks_ref), (own_hbm, own_ref), (mask_hbm, mask_ref), (far_hbm, far_ref)]
+            [(x_hbm.at[:, at], x_ref.at[:, at]) for at in pieces]
+            + [(picks_hbm, picks_ref), (own_hbm, own_ref), (mask_hbm, mask_ref), (far_hbm, far_ref)]
         )
     ]
     for copy in copies:
         copy.start()
     bins, twice = turned.shape
-    for copy in copies[1:]:
+    for copy in copies[PIECES:]:
         copy.wait()
     row_ref[...] = jnp.where(mask_ref[...] > 0, own_ref[...], 2 * twice)
-    copies[0].wait()
+    for copy in copies[:PIECES]:
+        copy.wait()
     x = x_ref[0].astype(F32)
     turned[...] = jnp.concatenate([x[:, :bins], x[:, bins:]], axis=0).T
     by_parity = [turned[pl.ds(odd, bins // 2, stride=2), :] for odd in range(2)]
@@ -147,7 +152,7 @@
         ),
         [HBM] * 5,
         (VMEM,) * 4,
-        [pltpu.VMEM(a.shape, a.dtype) for a in (spectra, own, mask)] + [pltpu.VMEM((bins, 2 * stations), F32), dma((5,))],
+        [pltpu.VMEM(a.shape, a.dtype) for a in (spectra, own, mask)] + [pltpu.VMEM((bins, 2 * stations), F32), dma((4 + PIECES,))],
     )(*given)
     mine = lax.all_to_all(by_bin, "day", split_axis=0, concat_axis=0, tiled=True)
     chosen = call(pick_kernel, shape((n_sta, SLOTS, width), BF16), [VMEM] * 2, VMEM)(picks, mine)

time: 65.8 us -> 65.8 us (level)
  no operation moved by 1% of the time
where the time goes in v5:
time: 65.8 us; the launch traced here: 64.7 us
  blocking collectives  61.1 us (93%)
  Pallas kernels  3.5 us (5%)
    all_to_all x1, blocking collectives, local(): lax.all_to_all(chosen, 'sta', split_axis=0, concat_axis=0, tiled=True)  27.3 us
    all_to_all x1, blocking collectives, local(): lax.all_to_all(by_bin, 'day', split_axis=0, concat_axis=0, tiled=True)  18.5 us
    all_to_all x1, blocking collectives, local(): lax.all_to_all(cross, 'day', split_axis=0, concat_axis=0, tiled=True)  15.3 us

profile of v5, /device:TPU:6, one launch (start us, length us, event | category | flops | bytes accessed | tf_op | source)
XLA Modules:
  0.0 64.7 jit_solution(5971174551960834432)
XLA Ops:
  0.0 1.0 %shard_map.73 = (bf16[8,32,128]{2,1,0:T(8,128)(2,1)S(1)}, s32[8,64]{1,0:T(8,128)S(1)}, s32[8,128]{1,0:T(8,128)S(1)}, s32[8,128]{1,0:T(8,128)S(1)}) custom-call(bf16[1,64,512]{2,1,0:T(8,128)(2,1)} %x_hbm.1, s32[8,64]{1,0:T(8,128)} %bitcast.10, s32[8,128]{1,0:T(8,128)} %bitcast.11, s32[8,128]{1,0:T(8,128)} %bitcast.12, s32[8,128]{1,0:T(8,128)} %bitcast.13), custom_call_target="tpu_custom_call" | custom-call | tf_op jit(solution)/shard_map/pallas_call | solution.py:145
  1.0 18.5 %all_to_all.15.mine_ref = bf16[8,32,128]{2,1,0:T(8,128)(2,1)S(1)} all-to-all(bf16[8,32,128]{2,1,0:T(8,128)(2,1)S(1)} %get-tuple-element.11), channel_id=1, replica_groups=mesh['sta'=64,'day'=8] {'day'}, dimensions={0} | all-to-all | bytes 131072 | tf_op jit(solution)/shard_map/all_to_all | solution.py:157
  19.5 0.4 shard_map.74
  19.8 27.3 %all_to_all.16 = bf16[64,8,512]{2,1,0:T(8,128)(2,1)S(1)} all-to-all(bf16[64,8,512]{2,1,0:T(8,128)(2,1)S(1)} %shard_map.74), channel_id=1, replica_groups=mesh['sta'=64,'day'=8] {'sta'}, dimensions={0} | all-to-all | bytes 1048576 | tf_op jit(solution)/shard_map/all_to_all | solution.py:159
  47.1 0.0 copy-start
  47.1 0.0 copy-start.1
  47.1 1.0 %shard_map.75 = f32[8,64,128]{2,1,0:T(8,128)S(1)} custom-call(s32[8,128]{1,0:T(8,128)S(1)} %get-tuple-element.9.own_ref, s32[8,128]{1,0:T(8,128)S(1)} %get-tuple-element.10.far_ref, bf16[8,32,128]{2,1,0:T(8,128)(2,1)S(1)} %all_to_all.15.mine_ref, bf16[512,512]{1,0:T(8,128)(2,1)S(1)} %bitcast.8), custom_call_target="tpu_custom_call" | custom-call | tf_op jit(solution)/shard_map/pallas_call | solution.py:160
  48.2 15.3 %all_to_all.17 = f32[8,64,128]{2,1,0:T(8,128)S(1)} all-to-all(f32[8,64,128]{2,1,0:T(8,128)S(1)} %shard_map.75), channel_id=1, replica_groups=mesh['sta'=64,'day'=8] {'day'}, dimensions={0} | all-to-all | bytes 524288 | tf_op jit(solution)/shard_map/all_to_all | solution.py:167
  63.5 0.0 copy-done
  63.5 0.0 copy-done.1
  63.5 1.2 %shard_map.76 = f32[128,1024]{1,0:T(8,128)} custom-call(f32[512,128]{1,0:T(8,128)S(1)} %bitcast.9, bf16[512,512]{1,0:T(8,128)(2,1)S(1)} %copy-done.1, bf16[512,512]{1,0:T(8,128)(2,1)S(1)} %copy-done), custom_call_target="tpu_custom_call" | custom-call | tf_op jit(solution)/shard_map/pallas_call | solution.py:169
Async XLA Ops:
  47.1 16.4 %copy-start = (bf16[512,512]{1,0:T(8,128)(2,1)S(1)}, bf16[512,512]{1,0:T(8,128)(2,1)}, u32[]{:S(2)}) copy-start(bf16[512,512]{1,0:T(8,128)(2,1)} %constant.5.clone.low_ref) | copy-start | bytes 1572868
  47.1 16.4 %copy-start.1 = (bf16[512,512]{1,0:T(8,128)(2,1)S(1)}, bf16[512,512]{1,0:T(8,128)(2,1)}, u32[]{:S(2)}) copy-start(bf16[512,512]{1,0:T(8,128)(2,1)} %constant.4.clone.high_ref) | copy-start | bytes 1572868
